TPU v7x, 512 devices: a whole 4x4x16 slice. The times are simulated.
512 devices in a mesh: sector: 16 (over z), chan: 32 (over x, y, core).
Axes of the slice: x: 4, y: 4, z: 16, core: 2. Of those that a mesh axis runs over, the one named last changes fastest.
Arguments:
- angular: bfloat16 [2048, 2048], P(None, 'chan'), may hold values from -0.125 to 0.125
- potential: float32 [32, 2048], replicated, may hold values from 0.25 to 4
- point_rows: int32 [32], replicated, may hold values from 0 to 31, each once
- quanta: int32 [2, 2048], P(None, 'chan'), may hold values from 0 to 7
- start_waves: float32 [48, 2048], P(None, 'chan'), may hold values from -6 to 6
Outputs:
- waves: float32 [32, 48, 2048], P('sector', None, 'chan')
Inputs may be any that keep to these rules, and one draw needn't show every extreme that they name: `point_rows`: A permutation: each row of potential belongs to exactly one radial point.
All inputs are finite; a program needn't handle non-finite values.
Results may differ from a plain program's by a relative error of at most 0.014.
Values may be sent and summed in bfloat16 or wider, within the bound.
A program may use at most 64 MiB of HBM per device.

v0:
```python
import jax
import jax.numpy as jnp
from jax import lax
from jax.sharding import PartitionSpec as P

energy = 3.5
rotor_const = 0.02
radius_first = 8.0
radius_step = 0.5
step_square = 0.08


def from_behind(block, axis, distance):
    devices = range(lax.axis_size(axis))
    route = [(i - distance, i) for i in devices if i - distance in devices]
    return lax.ppermute(block, axis, route)


def level_rows(j_values, l_values, radius):
    return (
        energy
        - rotor_const * j_values[None, :] * (j_values[None, :] + 1.0)
        - (l_values * (l_values + 1.0))[None, :] / (radius * radius)[:, None]
    )


def local(angular, potential, point_rows, quanta, start_waves):
    sector = lax.axis_index("sector")
    sector_count = lax.axis_size("sector")
    first_point = 2 * sector
    picked = lax.dynamic_slice_in_dim(point_rows, first_point, 2)
    root_pot = jnp.sqrt(jnp.take(potential, picked, axis=0))
    scaled_mine = (root_pot[:, :, None] * angular[None].astype(jnp.float32)).astype(jnp.bfloat16)
    scaled_piece = (
        root_pot[:, :, None]
        * lax.all_gather(angular, "chan", axis=1, tiled=True)[None].astype(jnp.float32)
    ).astype(jnp.bfloat16)
    coupling = jnp.einsum(
        "pqa,pqb->pab", scaled_mine, scaled_piece, preferred_element_type=jnp.float32
    ).astype(jnp.bfloat16)
    j_values = quanta[0].astype(jnp.float32)
    l_values = quanta[1].astype(jnp.float32)
    radius = radius_first + radius_step * (first_point + jnp.arange(2, dtype=jnp.int32)).astype(
        jnp.float32
    )
    levels = level_rows(j_values, l_values, radius)

    def advance(earlier, current, point_index):
        gathered = lax.all_gather(current.astype(jnp.bfloat16), "chan", axis=1, tiled=True)
        coupled = lax.dot_general(
            gathered,
            coupling[point_index],
            (((1,), (1,)), ((), ())),
            preferred_element_type=jnp.float32,
        )
        return (
            (2.0 - step_square * levels[point_index])[None, :] * current
            - earlier
            - step_square * coupled
        )

    def section(earlier, current):
        first_wave = advance(earlier, current, 0)
        second_wave = advance(current, first_wave, 1)
        return jnp.stack([first_wave, second_wave])

    def sweep(section_index, carry):
        earlier, current, collected = carry
        pair = section(earlier, current)
        collected = jnp.where(sector == section_index, pair, collected)
        arrived = from_behind(pair, "sector", 1)
        return (arrived[0], arrived[1], collected)

    blank = jnp.zeros((2,) + start_waves.shape, jnp.float32)
    earlier, current, collected = lax.fori_loop(
        0, sector_count - 1, sweep, (jnp.zeros_like(start_waves), start_waves, blank)
    )
    pair = section(earlier, current)
    return jnp.where(sector == sector_count - 1, pair, collected)


def solution(mesh):
    placed = (P(None, "chan"), P(), P(), P(None, "chan"), P(None, "chan"))
    return jax.shard_map(
        local, mesh=mesh, in_specs=placed, out_specs=P("sector", None, "chan"), check_vma=False
    )
```

profile of v0, /device:TPU:481, one launch (start us, length us, event | category | flops | bytes accessed | tf_op | source)
XLA Modules:
  0.0 982.8 jit_solution(5626338809701295255)
XLA Ops:
  10.6 67.6 %all-gather.12.cloned.1.call-done = bf16[2048,2048]{0,1:T(8,128)(2,1)} async-done(((bf16[2048,64]{0,1:T(8,128)(2,1)}), bf16[2048,2048]{0,1:T(8,128)(2,1)}) %all-gather.12.cloned.1.call-update) | async-done | bytes 8388624 | tf_op jit(solution)/shard_map/all_gather | solution.py:36
  78.2 13.1 %copy.14 = f32[2048,2048]{1,0:T(8,128)} copy(bf16[2048,2048]{0,1:T(8,128)(2,1)} %all-gather.12.cloned.1.call-done) | data formatting | bytes 25165824 | tf_op jit(solution)/shard_map/convert_element_type | solution.py:36
  91.2 8.9 fusion.10
  100.1 826.4 %while.18 = (s32[]{:T(128)}, f32[48,64]{1,0:T(8,128)S(1)}, f32[48,64]{1,0:T(8,128)S(1)}, f32[2,48,64]{2,1,0:T(8,128)S(1)}, f32[2,64]{1,0:T(2,128)S(1)}, /*index=...) while((s32[]{:T(128)}, f32[48,64]{1,0:T(8,128)S(1)}, f32[48,64]{1,0:T(8,128)S(1)}, ...), condition=%wide.region_1.2_spmd.clone, body=%wide.region_0.1_spmd.clone.sunk | while | flops 25215236 | bytes 3303577 | solution.py:75
  100.2 24.6 %all-gather.8 = bf16[32,64,48]{1,2,0:T(8,128)(2,1)S(1)} all-gather(bf16[1,64,48]{1,2,0:T(8,128)(2,1)S(1)} %convert_bitcast_fusion.6), channel_id=1, replica_groups=mesh['sector'=16,'chan'=32] {'chan'}, dimensions={0}, use_global_device_ids=true | all-gather | bytes 202752 | tf_op jit(solution)/shard_map/while/body/eval_jaxpr/all_gather | solution.py:49
  125.4 22.6 %all-gather.9 = bf16[32,64,48]{1,2,0:T(8,128)(2,1)S(1)} all-gather(bf16[1,64,48]{1,2,0:T(8,128)(2,1)S(1)} %convert_bitcast_fusion.7), channel_id=1, replica_groups=mesh['sector'=16,'chan'=32] {'chan'}, dimensions={0}, use_global_device_ids=true | all-gather | bytes 202752 | tf_op jit(solution)/shard_map/while/body/eval_jaxpr/all_gather | solution.py:49
  148.8 1.3 collective-permute-start
  150.1 3.5 collective-permute-done
  153.6 25.3 %all-gather.8 = bf16[32,64,48]{1,2,0:T(8,128)(2,1)S(1)} all-gather(bf16[1,64,48]{1,2,0:T(8,128)(2,1)S(1)} %convert_bitcast_fusion.6), channel_id=1, replica_groups=mesh['sector'=16,'chan'=32] {'chan'}, dimensions={0}, use_global_device_ids=true | all-gather | bytes 202752 | tf_op jit(solution)/shard_map/while/body/eval_jaxpr/all_gather | solution.py:49
  179.7 22.6 %all-gather.9 = bf16[32,64,48]{1,2,0:T(8,128)(2,1)S(1)} all-gather(bf16[1,64,48]{1,2,0:T(8,128)(2,1)S(1)} %convert_bitcast_fusion.7), channel_id=1, replica_groups=mesh['sector'=16,'chan'=32] {'chan'}, dimensions={0}, use_global_device_ids=true | all-gather | bytes 202752 | tf_op jit(solution)/shard_map/while/body/eval_jaxpr/all_gather | solution.py:49
  203.0 1.3 collective-permute-start
  204.3 3.5 collective-permute-done
  207.9 25.3 %all-gather.8 = bf16[32,64,48]{1,2,0:T(8,128)(2,1)S(1)} all-gather(bf16[1,64,48]{1,2,0:T(8,128)(2,1)S(1)} %convert_bitcast_fusion.6), channel_id=1, replica_groups=mesh['sector'=16,'chan'=32] {'chan'}, dimensions={0}, use_global_device_ids=true | all-gather | bytes 202752 | tf_op jit(solution)/shard_map/while/body/eval_jaxpr/all_gather | solution.py:49
  233.9 22.6 %all-gather.9 = bf16[32,64,48]{1,2,0:T(8,128)(2,1)S(1)} all-gather(bf16[1,64,48]{1,2,0:T(8,128)(2,1)S(1)} %convert_bitcast_fusion.7), channel_id=1, replica_groups=mesh['sector'=16,'chan'=32] {'chan'}, dimensions={0}, use_global_device_ids=true | all-gather | bytes 202752 | tf_op jit(solution)/shard_map/while/body/eval_jaxpr/all_gather | solution.py:49
  257.2 1.3 collective-permute-start
  258.5 3.5 collective-permute-done
  262.1 25.3 %all-gather.8 = bf16[32,64,48]{1,2,0:T(8,128)(2,1)S(1)} all-gather(bf16[1,64,48]{1,2,0:T(8,128)(2,1)S(1)} %convert_bitcast_fusion.6), channel_id=1, replica_groups=mesh['sector'=16,'chan'=32] {'chan'}, dimensions={0}, use_global_device_ids=true | all-gather | bytes 202752 | tf_op jit(solution)/shard_map/while/body/eval_jaxpr/all_gather | solution.py:49
  288.1 22.6 %all-gather.9 = bf16[32,64,48]{1,2,0:T(8,128)(2,1)S(1)} all-gather(bf16[1,64,48]{1,2,0:T(8,128)(2,1)S(1)} %convert_bitcast_fusion.7), channel_id=1, replica_groups=mesh['sector'=16,'chan'=32] {'chan'}, dimensions={0}, use_global_device_ids=true | all-gather | bytes 202752 | tf_op jit(solution)/shard_map/while/body/eval_jaxpr/all_gather | solution.py:49
  311.5 1.3 collective-permute-start
  312.8 3.5 collective-permute-done
  316.3 25.3 %all-gather.8 = bf16[32,64,48]{1,2,0:T(8,128)(2,1)S(1)} all-gather(bf16[1,64,48]{1,2,0:T(8,128)(2,1)S(1)} %convert_bitcast_fusion.6), channel_id=1, replica_groups=mesh['sector'=16,'chan'=32] {'chan'}, dimensions={0}, use_global_device_ids=true | all-gather | bytes 202752 | tf_op jit(solution)/shard_map/while/body/eval_jaxpr/all_gather | solution.py:49
  342.3 22.6 %all-gather.9 = bf16[32,64,48]{1,2,0:T(8,128)(2,1)S(1)} all-gather(bf16[1,64,48]{1,2,0:T(8,128)(2,1)S(1)} %convert_bitcast_fusion.7), channel_id=1, replica_groups=mesh['sector'=16,'chan'=32] {'chan'}, dimensions={0}, use_global_device_ids=true | all-gather | bytes 202752 | tf_op jit(solution)/shard_map/while/body/eval_jaxpr/all_gather | solution.py:49
  365.7 1.3 collective-permute-start
  367.0 5.2 collective-permute-done
  372.1 24.8 %all-gather.8 = bf16[32,64,48]{1,2,0:T(8,128)(2,1)S(1)} all-gather(bf16[1,64,48]{1,2,0:T(8,128)(2,1)S(1)} %convert_bitcast_fusion.6), channel_id=1, replica_groups=mesh['sector'=16,'chan'=32] {'chan'}, dimensions={0}, use_global_device_ids=true | all-gather | bytes 202752 | tf_op jit(solution)/shard_map/while/body/eval_jaxpr/all_gather | solution.py:49
  397.6 22.6 %all-gather.9 = bf16[32,64,48]{1,2,0:T(8,128)(2,1)S(1)} all-gather(bf16[1,64,48]{1,2,0:T(8,128)(2,1)S(1)} %convert_bitcast_fusion.7), channel_id=1, replica_groups=mesh['sector'=16,'chan'=32] {'chan'}, dimensions={0}, use_global_device_ids=true | all-gather | bytes 202752 | tf_op jit(solution)/shard_map/while/body/eval_jaxpr/all_gather | solution.py:49
  421.0 1.3 collective-permute-start
  422.3 5.3 collective-permute-done
  427.6 24.8 %all-gather.8 = bf16[32,64,48]{1,2,0:T(8,128)(2,1)S(1)} all-gather(bf16[1,64,48]{1,2,0:T(8,128)(2,1)S(1)} %convert_bitcast_fusion.6), channel_id=1, replica_groups=mesh['sector'=16,'chan'=32] {'chan'}, dimensions={0}, use_global_device_ids=true | all-gather | bytes 202752 | tf_op jit(solution)/shard_map/while/body/eval_jaxpr/all_gather | solution.py:49
  453.1 22.6 %all-gather.9 = bf16[32,64,48]{1,2,0:T(8,128)(2,1)S(1)} all-gather(bf16[1,64,48]{1,2,0:T(8,128)(2,1)S(1)} %convert_bitcast_fusion.7), channel_id=1, replica_groups=mesh['sector'=16,'chan'=32] {'chan'}, dimensions={0}, use_global_device_ids=true | all-gather | bytes 202752 | tf_op jit(solution)/shard_map/while/body/eval_jaxpr/all_gather | solution.py:49
  476.4 1.3 collective-permute-start
  477.7 5.3 collective-permute-done
  483.0 24.8 %all-gather.8 = bf16[32,64,48]{1,2,0:T(8,128)(2,1)S(1)} all-gather(bf16[1,64,48]{1,2,0:T(8,128)(2,1)S(1)} %convert_bitcast_fusion.6), channel_id=1, replica_groups=mesh['sector'=16,'chan'=32] {'chan'}, dimensions={0}, use_global_device_ids=true | all-gather | bytes 202752 | tf_op jit(solution)/shard_map/while/body/eval_jaxpr/all_gather | solution.py:49
  508.5 22.6 %all-gather.9 = bf16[32,64,48]{1,2,0:T(8,128)(2,1)S(1)} all-gather(bf16[1,64,48]{1,2,0:T(8,128)(2,1)S(1)} %convert_bitcast_fusion.7), channel_id=1, replica_groups=mesh['sector'=16,'chan'=32] {'chan'}, dimensions={0}, use_global_device_ids=true | all-gather | bytes 202752 | tf_op jit(solution)/shard_map/while/body/eval_jaxpr/all_gather | solution.py:49
  531.8 1.3 collective-permute-start
  533.1 5.3 collective-permute-done
  538.5 24.8 %all-gather.8 = bf16[32,64,48]{1,2,0:T(8,128)(2,1)S(1)} all-gather(bf16[1,64,48]{1,2,0:T(8,128)(2,1)S(1)} %convert_bitcast_fusion.6), channel_id=1, replica_groups=mesh['sector'=16,'chan'=32] {'chan'}, dimensions={0}, use_global_device_ids=true | all-gather | bytes 202752 | tf_op jit(solution)/shard_map/while/body/eval_jaxpr/all_gather | solution.py:49
  563.9 22.6 %all-gather.9 = bf16[32,64,48]{1,2,0:T(8,128)(2,1)S(1)} all-gather(bf16[1,64,48]{1,2,0:T(8,128)(2,1)S(1)} %convert_bitcast_fusion.7), channel_id=1, replica_groups=mesh['sector'=16,'chan'=32] {'chan'}, dimensions={0}, use_global_device_ids=true | all-gather | bytes 202752 | tf_op jit(solution)/shard_map/while/body/eval_jaxpr/all_gather | solution.py:49
  587.3 1.3 collective-permute-start
  588.6 5.3 collective-permute-done
  593.9 24.8 %all-gather.8 = bf16[32,64,48]{1,2,0:T(8,128)(2,1)S(1)} all-gather(bf16[1,64,48]{1,2,0:T(8,128)(2,1)S(1)} %convert_bitcast_fusion.6), channel_id=1, replica_groups=mesh['sector'=16,'chan'=32] {'chan'}, dimensions={0}, use_global_device_ids=true | all-gather | bytes 202752 | tf_op jit(solution)/shard_map/while/body/eval_jaxpr/all_gather | solution.py:49
  619.4 22.6 %all-gather.9 = bf16[32,64,48]{1,2,0:T(8,128)(2,1)S(1)} all-gather(bf16[1,64,48]{1,2,0:T(8,128)(2,1)S(1)} %convert_bitcast_fusion.7), channel_id=1, replica_groups=mesh['sector'=16,'chan'=32] {'chan'}, dimensions={0}, use_global_device_ids=true | all-gather | bytes 202752 | tf_op jit(solution)/shard_map/while/body/eval_jaxpr/all_gather | solution.py:49
  642.7 1.3 collective-permute-start
  644.0 5.3 collective-permute-done
  649.3 24.8 %all-gather.8 = bf16[32,64,48]{1,2,0:T(8,128)(2,1)S(1)} all-gather(bf16[1,64,48]{1,2,0:T(8,128)(2,1)S(1)} %convert_bitcast_fusion.6), channel_id=1, replica_groups=mesh['sector'=16,'chan'=32] {'chan'}, dimensions={0}, use_global_device_ids=true | all-gather | bytes 202752 | tf_op jit(solution)/shard_map/while/body/eval_jaxpr/all_gather | solution.py:49
  674.8 22.6 %all-gather.9 = bf16[32,64,48]{1,2,0:T(8,128)(2,1)S(1)} all-gather(bf16[1,64,48]{1,2,0:T(8,128)(2,1)S(1)} %convert_bitcast_fusion.7), channel_id=1, replica_groups=mesh['sector'=16,'chan'=32] {'chan'}, dimensions={0}, use_global_device_ids=true | all-gather | bytes 202752 | tf_op jit(solution)/shard_map/while/body/eval_jaxpr/all_gather | solution.py:49
  698.1 1.3 collective-permute-start
  699.4 5.3 collective-permute-done
  704.8 24.8 %all-gather.8 = bf16[32,64,48]{1,2,0:T(8,128)(2,1)S(1)} all-gather(bf16[1,64,48]{1,2,0:T(8,128)(2,1)S(1)} %convert_bitcast_fusion.6), channel_id=1, replica_groups=mesh['sector'=16,'chan'=32] {'chan'}, dimensions={0}, use_global_device_ids=true | all-gather | bytes 202752 | tf_op jit(solution)/shard_map/while/body/eval_jaxpr/all_gather | solution.py:49
  730.2 22.6 %all-gather.9 = bf16[32,64,48]{1,2,0:T(8,128)(2,1)S(1)} all-gather(bf16[1,64,48]{1,2,0:T(8,128)(2,1)S(1)} %convert_bitcast_fusion.7), channel_id=1, replica_groups=mesh['sector'=16,'chan'=32] {'chan'}, dimensions={0}, use_global_device_ids=true | all-gather | bytes 202752 | tf_op jit(solution)/shard_map/while/body/eval_jaxpr/all_gather | solution.py:49
  753.6 1.3 collective-permute-start
  754.9 5.3 collective-permute-done
  760.2 24.8 %all-gather.8 = bf16[32,64,48]{1,2,0:T(8,128)(2,1)S(1)} all-gather(bf16[1,64,48]{1,2,0:T(8,128)(2,1)S(1)} %convert_bitcast_fusion.6), channel_id=1, replica_groups=mesh['sector'=16,'chan'=32] {'chan'}, dimensions={0}, use_global_device_ids=true | all-gather | bytes 202752 | tf_op jit(solution)/shard_map/while/body/eval_jaxpr/all_gather | solution.py:49
  785.7 22.6 %all-gather.9 = bf16[32,64,48]{1,2,0:T(8,128)(2,1)S(1)} all-gather(bf16[1,64,48]{1,2,0:T(8,128)(2,1)S(1)} %convert_bitcast_fusion.7), channel_id=1, replica_groups=mesh['sector'=16,'chan'=32] {'chan'}, dimensions={0}, use_global_device_ids=true | all-gather | bytes 202752 | tf_op jit(solution)/shard_map/while/body/eval_jaxpr/all_gather | solution.py:49
  809.0 1.3 collective-permute-start
  810.3 5.3 collective-permute-done
  815.6 24.8 %all-gather.8 = bf16[32,64,48]{1,2,0:T(8,128)(2,1)S(1)} all-gather(bf16[1,64,48]{1,2,0:T(8,128)(2,1)S(1)} %convert_bitcast_fusion.6), channel_id=1, replica_groups=mesh['sector'=16,'chan'=32] {'chan'}, dimensions={0}, use_global_device_ids=true | all-gather | bytes 202752 | tf_op jit(solution)/shard_map/while/body/eval_jaxpr/all_gather | solution.py:49
  841.1 22.6 %all-gather.9 = bf16[32,64,48]{1,2,0:T(8,128)(2,1)S(1)} all-gather(bf16[1,64,48]{1,2,0:T(8,128)(2,1)S(1)} %convert_bitcast_fusion.7), channel_id=1, replica_groups=mesh['sector'=16,'chan'=32] {'chan'}, dimensions={0}, use_global_device_ids=true | all-gather | bytes 202752 | tf_op jit(solution)/shard_map/while/body/eval_jaxpr/all_gather | solution.py:49
  865.7 5.3 collective-permute-done
  871.1 24.8 %all-gather.8 = bf16[32,64,48]{1,2,0:T(8,128)(2,1)S(1)} all-gather(bf16[1,64,48]{1,2,0:T(8,128)(2,1)S(1)} %convert_bitcast_fusion.6), channel_id=1, replica_groups=mesh['sector'=16,'chan'=32] {'chan'}, dimensions={0}, use_global_device_ids=true | all-gather | bytes 202752 | tf_op jit(solution)/shard_map/while/body/eval_jaxpr/all_gather | solution.py:49
  896.5 22.6 %all-gather.9 = bf16[32,64,48]{1,2,0:T(8,128)(2,1)S(1)} all-gather(bf16[1,64,48]{1,2,0:T(8,128)(2,1)S(1)} %convert_bitcast_fusion.7), channel_id=1, replica_groups=mesh['sector'=16,'chan'=32] {'chan'}, dimensions={0}, use_global_device_ids=true | all-gather | bytes 202752 | tf_op jit(solution)/shard_map/while/body/eval_jaxpr/all_gather | solution.py:49
  921.2 5.3 collective-permute-done
  926.5 24.8 %all-gather.2 = bf16[32,64,48]{1,2,0:T(8,128)(2,1)S(1)} all-gather(bf16[1,64,48]{1,2,0:T(8,128)(2,1)S(1)} %convert_bitcast_fusion.3), channel_id=1, replica_groups=mesh['sector'=16,'chan'=32] {'chan'}, dimensions={0}, use_global_device_ids=true | all-gather | bytes 202752 | tf_op jit(solution)/shard_map/all_gather | solution.py:49
  952.0 22.6 %all-gather.3 = bf16[32,64,48]{1,2,0:T(8,128)(2,1)S(1)} all-gather(bf16[1,64,48]{1,2,0:T(8,128)(2,1)S(1)} %convert_bitcast_fusion.2), channel_id=1, replica_groups=mesh['sector'=16,'chan'=32] {'chan'}, dimensions={0}, use_global_device_ids=true | all-gather | bytes 202752 | tf_op jit(solution)/shard_map/all_gather | solution.py:49
  (193 shorter events, 29.3 us)
Async XLA Ops:
  6.5 2.5 copy-start
  6.5 71.6 %all-gather.12.cloned.1.call-start = ((), (), s32[]{:S(2)}) async-start(), calls=%async_computation | async-start | bytes 8650752 | tf_op jit(solution)/shard_map/all_gather | solution.py:36
  91.2 8.9 copy-start.1
  148.8 4.8 collective-permute-start
  203.0 4.8 collective-permute-start
  257.2 4.8 collective-permute-start
  311.5 4.8 collective-permute-start
  365.7 6.5 collective-permute-start
  421.0 6.6 collective-permute-start
  476.4 6.6 collective-permute-start
  531.8 6.6 collective-permute-start
  587.3 6.6 collective-permute-start
  642.7 6.6 collective-permute-start
  698.1 6.6 collective-permute-start
  753.6 6.6 collective-permute-start
  809.0 6.6 collective-permute-start
  864.4 6.6 collective-permute-start
  919.9 6.6 collective-permute-start
Sparse Core Ops, SparseCore 0:
  10.5 67.6 all-gather.11
where the time goes:
time: 993 us; the launch traced here: 983 us
  blocking collectives  760 us (77%)
  waiting for transfers between devices  141 us (14%)
  local copies, waits for them, and re-layouts  28.5 us (3%)
  starting transfers between devices  19.4 us (2%)
  matrix products  15.6 us (2%)
  between operations  13.5 us (1%)
    all_gather x32, blocking collectives, advance(): lax.all_gather(current.astype(jnp.bfloat16), 'chan', axis=1, tiled=True)  760 us
    ppermute x15, waiting for transfers between devices, from_behind(): return lax.ppermute(block, axis, route)  72.5 us
    all_gather x1, waiting for transfers between devices, local(): lax.all_gather(angular, 'chan', axis=1, tiled=True)[None]  67.6 us
  transfers between devices with their start and end apart: 16, of which 16 were waited for; matrix products, arithmetic and copies ran while one was open for 0% of the time, Pallas kernels for 0%

commit v1 on v0

v1 whole, which is shorter than its diff:
```python
import functools

import jax
import jax.numpy as jnp
from jax import lax
from jax.experimental import pallas as pl
from jax.experimental.pallas import tpu as pltpu
from jax.sharding import PartitionSpec as P

energy = 3.5
rotor_const = 0.02
radius_first = 8.0
radius_step = 0.5
step_square = 0.08

GROUPS = (5, 5, 6)
TILE = 512
MESH = pl.DeviceIdType.MESH


def pick(index, values):
    result = values[-1]
    for place in range(len(values) - 1):
        result = jnp.where(index == place, values[place], result)
    return result


def kernel(
    chans, sectors,
    full_ref, rows_ref, pot_ref, quanta_ref, start_ref, out_ref,
    basis, flipped, state, rounded, weighted, turned,
    whole, message, terms, table, level_send, level_recv, wave_send, wave_recv, hop_send, hop_recv, load_sem,
):
    n = basis.shape[0]
    width = n // chans
    solutions = start_ref.shape[0]
    sector, me = lax.axis_index("sector"), lax.axis_index("chan")
    group_of, first_of, last_of, next_of = [], [], [], []
    start = 0
    for index, size in enumerate(GROUPS):
        following = GROUPS[index + 1] if index + 1 < len(GROUPS) else 0
        for _ in range(size):
            first_of.append(start)
            last_of.append(start + size - 1)
            next_of.append(following)
        start += size
    first = pick(sector, first_of)
    last = pick(sector, last_of)
    following = pick(sector, next_of)
    sends = jnp.logical_and(sector == last, following > 0)
    previous = first - 1

    load = pltpu.make_async_copy(full_ref, basis, load_sem)
    load.start()

    barrier = pltpu.get_barrier_semaphore()

    def greet(distance, carry):
        peer = lax.rem(me + distance, chans)
        pl.semaphore_signal(barrier, inc=1, device_id=(sector, peer), device_id_type=MESH)
        return carry

    lax.fori_loop(1, chans, greet, 0)

    @pl.when(sends)
    def _():
        def greet_next(step, carry):
            pl.semaphore_signal(barrier, inc=1, device_id=(sector + 1 + step, me), device_id_type=MESH)
            return carry

        lax.fori_loop(0, following, greet_next, 0)

    @pl.when(first > 0)
    def _():
        pl.semaphore_signal(barrier, inc=1, device_id=(previous, me), device_id_type=MESH)

    greeted = chans - 1 + jnp.where(sends, following, 0) + jnp.where(first > 0, 1, 0)
    pl.semaphore_wait(barrier, greeted)

    quanta = quanta_ref[...].astype(jnp.float32)
    j_values, l_values = quanta[0:1, :], quanta[1:2, :]
    a_row = 2.0 - step_square * (energy - rotor_const * j_values * (j_values + 1.0))
    b_row = step_square * (l_values * (l_values + 1.0))
    ab = jnp.concatenate([a_row, b_row, jnp.zeros((6, width), jnp.float32)], axis=0)
    lane = lax.broadcasted_iota(jnp.int32, (8, 2 * width), 1)
    half = lane // width
    terms[me] = jnp.where(half == lax.rem(me, 2), jnp.concatenate([ab, ab], axis=1), 0.0)

    def level_copy(peer):
        return pltpu.make_async_remote_copy(
            src_ref=terms.at[me], dst_ref=terms.at[me],
            send_sem=level_send.at[peer], recv_sem=level_recv.at[me],
            device_id=(sector, peer), device_id_type=MESH,
        )

    def wave_slot(owner):
        return whole.at[:, pl.ds(pl.multiple_of(owner * 2 * width, 2 * width), 2 * width)]

    def wave_copy(peer):
        return pltpu.make_async_remote_copy(
            src_ref=wave_slot(me), dst_ref=wave_slot(me),
            send_sem=wave_send.at[peer], recv_sem=wave_recv.at[me],
            device_id=(sector, peer), device_id_type=MESH,
        )

    def to_peers(make):
        def go(distance, carry):
            make(lax.rem(me + distance, chans)).start()
            return carry

        lax.fori_loop(1, chans, go, 0)

    def sent_to_peers(make):
        def go(distance, carry):
            make(lax.rem(me + distance, chans)).wait_send()
            return carry

        lax.fori_loop(1, chans, go, 0)

    to_peers(level_copy)

    @pl.when(first == 0)
    def _():
        waves = start_ref[...].astype(jnp.bfloat16)
        whole[:, pl.ds(pl.multiple_of(me * 2 * width, 2 * width), 2 * width)] = jnp.concatenate(
            [waves, waves], axis=1
        )
        to_peers(wave_copy)

    load.wait()

    @pl.loop(0, n // 128)
    def _(block):
        rows = pl.ds(pl.multiple_of(block * 128, 128), 128)

        @pl.loop(0, n // TILE)
        def _(tile):
            columns = pl.ds(pl.multiple_of(tile * TILE, TILE), TILE)
            flipped[columns, rows] = jnp.transpose(basis[rows, columns])

    def level_wait(distance, carry):
        owner = lax.rem(me + distance, chans)
        pltpu.make_async_remote_copy(
            src_ref=terms.at[owner], dst_ref=terms.at[owner],
            send_sem=level_send.at[owner], recv_sem=level_recv.at[owner],
            device_id=(sector, owner), device_id_type=MESH,
        ).wait_recv()
        return carry

    lax.fori_loop(1, chans, level_wait, 0)

    @pl.loop(0, chans // 2)
    def _(pair):
        table[:, pl.ds(pl.multiple_of(pair * 128, 128), 128)] = terms[2 * pair] + terms[2 * pair + 1]

    top = 2 * sector + 1
    bottom = 2 * first

    @pl.loop(0, n // TILE)
    def _(tile):
        columns = pl.ds(pl.multiple_of(tile * TILE, TILE), TILE)
        shape = (2 * width, TILE)
        row = lax.broadcasted_iota(jnp.int32, shape, 0)
        column = lax.broadcasted_iota(jnp.int32, shape, 1) + tile * TILE
        later = row < width
        own = column == me * width + jnp.where(later, row, row - width)
        now = jnp.where(jnp.logical_and(own, later), 1.0, 0.0)
        state[0, :, columns] = now
        state[1, :, columns] = jnp.where(jnp.logical_and(own, jnp.logical_not(later)), -1.0, 0.0)
        rounded[:, columns] = now.astype(jnp.bfloat16)

    def back(step, carry):
        point = top - step
        current, other = lax.rem(step, 2), 1 - lax.rem(step, 2)
        row = rows_ref[point]

        @pl.loop(0, n // TILE)
        def _(tile):
            columns = pl.ds(pl.multiple_of(tile * TILE, TILE), TILE)
            product = jnp.dot(rounded[...], basis[:, columns], preferred_element_type=jnp.float32)
            weighted[:, columns] = (product * pot_ref[pl.ds(row, 1), columns]).astype(jnp.bfloat16)

        radius = jnp.full((1, TILE), radius_first, jnp.float32) + radius_step * point.astype(jnp.float32)
        inverse = 1.0 / (radius * radius)

        @pl.loop(0, n // TILE)
        def _(tile):
            columns = pl.ds(pl.multiple_of(tile * TILE, TILE), TILE)
            product = jnp.dot(weighted[...], flipped[:, columns], preferred_element_type=jnp.float32)
            factor = table[0:1, columns] + table[1:2, columns] * inverse
            new = factor * state[current, :, columns] - state[other, :, columns] - step_square * product
            state[other, :, columns] = new
            rounded[:, columns] = new.astype(jnp.bfloat16)

        return carry

    steps = top - bottom + 1
    lax.fori_loop(0, steps, back, 0)
    newest, older = lax.rem(steps, 2), 1 - lax.rem(steps, 2)

    low = lax.broadcasted_iota(jnp.int32, (2 * width, 128), 1) < width

    def differences(rows):
        return jnp.concatenate([rows[:width], rows[:width] - rows[width:]], axis=0)

    @pl.loop(0, chans // 2)
    def _(pair):
        columns = pl.ds(pl.multiple_of(pair * 128, 128), 128)
        before = differences(state[older, :, columns])
        main = differences(state[newest, :, columns]) - before
        left = jnp.where(low, main, pltpu.roll(before, width, 1))
        right = jnp.where(low, pltpu.roll(main, width, 1), before)
        turned[pl.ds(pl.multiple_of(pair * 256, 256), 128), :] = jnp.transpose(left).astype(jnp.bfloat16)
        turned[pl.ds(pl.multiple_of(pair * 256 + 128, 128), 128), :] = jnp.transpose(right).astype(jnp.bfloat16)

    @pl.when(first > 0)
    def _():
        pltpu.make_async_remote_copy(
            src_ref=message, dst_ref=wave_slot(me), send_sem=hop_send.at[0], recv_sem=hop_recv,
            device_id=(previous, me), device_id_type=MESH,
        ).wait_recv()
        to_peers(wave_copy)

    def wave_wait(distance, carry):
        owner = lax.rem(me + distance, chans)
        pltpu.make_async_remote_copy(
            src_ref=wave_slot(owner), dst_ref=wave_slot(owner),
            send_sem=wave_send.at[owner], recv_sem=wave_recv.at[owner],
            device_id=(sector, owner), device_id_type=MESH,
        ).wait_recv()
        return carry

    lax.fori_loop(1, chans, wave_wait, 0)
    result = jnp.dot(whole[...], turned[...], preferred_element_type=jnp.float32)
    swapped = pltpu.roll(result, width, 1)

    def hop_copy(step):
        return pltpu.make_async_remote_copy(
            src_ref=message, dst_ref=wave_slot(me), send_sem=hop_send.at[step], recv_sem=hop_recv,
            device_id=(sector + 1 + step, me), device_id_type=MESH,
        )

    @pl.when(sends)
    def _():
        message[...] = result.astype(jnp.bfloat16)

        def go(step, carry):
            hop_copy(following - 1 - step).start()
            return carry

        lax.fori_loop(0, following, go, 0)

        def done(step, carry):
            hop_copy(step).wait_send()
            return carry

        lax.fori_loop(0, following, done, 0)

    out_ref[0] = (result - swapped)[:, :width]
    out_ref[1] = result[:, :width]
    sent_to_peers(level_copy)
    sent_to_peers(wave_copy)


def local(angular, potential, point_rows, quanta, start_waves):
    chans, sectors = lax.axis_size("chan"), lax.axis_size("sector")
    points, n = angular.shape[0], angular.shape[1] * chans
    solutions, width = start_waves.shape
    full = lax.all_gather(angular.T, "chan", axis=0, tiled=True)
    vmem = pl.BlockSpec(memory_space=pltpu.VMEM)
    return pl.pallas_call(
        functools.partial(kernel, chans, sectors),
        out_shape=jax.ShapeDtypeStruct((2, solutions, width), jnp.float32),
        in_specs=[
            pl.BlockSpec(memory_space=pl.ANY),
            pl.BlockSpec(memory_space=pltpu.SMEM),
            vmem, vmem, vmem,
        ],
        out_specs=vmem,
        scratch_shapes=[
            pltpu.VMEM((n, points), jnp.bfloat16),
            pltpu.VMEM((points, n), jnp.bfloat16),
            pltpu.VMEM((2, 2 * width, n), jnp.float32),
            pltpu.VMEM((2 * width, n), jnp.bfloat16),
            pltpu.VMEM((2 * width, points), jnp.bfloat16),
            pltpu.VMEM((2 * n, 2 * width), jnp.bfloat16),
            pltpu.VMEM((solutions, 2 * n), jnp.bfloat16),
            pltpu.VMEM((solutions, 2 * width), jnp.bfloat16),
            pltpu.VMEM((chans, 8, 2 * width), jnp.float32),
            pltpu.VMEM((8, n), jnp.float32),
            pltpu.SemaphoreType.DMA((chans,)),
            pltpu.SemaphoreType.DMA((chans,)),
            pltpu.SemaphoreType.DMA((chans,)),
            pltpu.SemaphoreType.DMA((chans,)),
            pltpu.SemaphoreType.DMA((max(GROUPS),)),
            pltpu.SemaphoreType.DMA,
            pltpu.SemaphoreType.DMA,
        ],
        compiler_params=pltpu.CompilerParams(
            collective_id=0, has_side_effects=True, vmem_limit_bytes=48 * 1024 * 1024
        ),
    )(full, point_rows, potential, quanta, start_waves)


def solution(mesh):
    placed = (P(None, "chan"), P(), P(), P(None, "chan"), P(None, "chan"))
    return jax.shard_map(
        local, mesh=mesh, in_specs=placed, out_specs=P("sector", None, "chan"), check_vma=False
    )
```

time: 993 us -> 173 us (0.17)
  blocking collectives: 760 us -> 0 us
  Pallas kernels: 0 us -> 84 us
  waiting for transfers between devices: 141 us -> 71.6 us
  local copies, waits for them, and re-layouts: 28.5 us -> 3.64 us
  starting transfers between devices: 19.4 us -> 0.01 us
  matrix products: 15.6 us -> 0 us
    all_gather x32 -> x0, blocking collectives: 760 us -> none  [advance(): lax.all_gather(current.astype(jnp.bfloat16), 'chan', axis=1, tiled=True)]
    pallas_call x0 -> x1, Pallas kernels: none -> 84 us  [local(): pl.pallas_call(functools.partial(kernel, chans, sectors), out_shape=jax.S...]
    ppermute x15 -> x0, waiting for transfers between devices: 72.5 us -> none  [from_behind(): return lax.ppermute(block, axis, route)]
    ppermute x15 -> x0, starting transfers between devices: 19.4 us -> none  [from_behind(): return lax.ppermute(block, axis, route)]
    dot_general x33 -> x0, matrix products: 15.6 us -> none  [the longest x1 8.87 us: local(): jnp.einsum('pqa,pqb->pab', scaled_mine, scaled_piece, preferred_element_t...]
    convert_element_type x1 -> x0, local copies, waits for them, and re-layouts: 13.1 us -> none  [local(): lax.all_gather(angular, 'chan', axis=1, tiled=True)[None]]
    while x30 -> x0, local copies, waits for them, and re-layouts: 10.8 us -> none
  transfers between devices with their start and end apart: 16 -> 1, of which waited for: 16 -> 1; matrix products, arithmetic and copies ran while one was open for 0% -> 0% of each run, Pallas kernels for 0% -> 0%
where the time goes in v1:
time: 173 us
  Pallas kernels  84 us (49%)
  waiting for transfers between devices  71.6 us (41%)
  between operations  13.4 us (8%)
  local copies, waits for them, and re-layouts  3.64 us (2%)
    pallas_call x1, Pallas kernels, local(): pl.pallas_call(functools.partial(kernel, chans, sectors), out_shape=jax.S...  84 us
    all_gather x1, waiting for transfers between devices, local(): full = lax.all_gather(angular.T, 'chan', axis=0, tiled=True)  70.9 us
    unnamed x9, local copies, waits for them, and re-layouts  3.64 us
  transfers between devices with their start and end apart: 1, of which 1 were waited for; matrix products, arithmetic and copies ran while one was open for 0% of the time, Pallas kernels for 0%

profile of v1, /device:TPU:481, one launch (start us, length us, event | category | flops | bytes accessed | tf_op | source)
XLA Modules:
  0.0 172.7 jit_solution(4739246736628139131)
XLA Ops:
  6.5 0.0 all-gather.2.cloned.1.call-start
  6.5 0.7 all-gather.2.cloned.1.call-update
  7.3 70.9 %all-gather.2.cloned.1.call-done.full_ref = bf16[2048,2048]{1,0:T(8,128)(2,1)} async-done(((bf16[64,2048]{1,0:T(8,128)(2,1)}), bf16[2048,2048]{1,0:T(8,128)(2,1)}) %all-gather.2.cloned.1.call-update) | async-done | bytes 8388624 | tf_op jit(solution)/shard_map/all_gather | solution.py:269
  78.2 0.0 copy-start
  78.2 0.9 copy-done
  79.1 0.0 copy-start.1
  79.1 0.7 copy-done.1
  79.9 0.0 copy-start.2
  79.9 0.7 copy-done.2
  80.5 0.0 copy-start.3
  80.5 0.7 copy-done.3
  81.2 84.0 %shard_map.55 = f32[2,48,64]{2,1,0:T(8,128)S(1)} custom-call(bf16[2048,2048]{1,0:T(8,128)(2,1)} %all-gather.2.cloned.1.call-done.full_ref, s32[32]{0:T(128)S(1)} %copy-done.3, f32[32,2048]{1,0:T(8,128)S(1)} %copy-done, s32[2,64]{1,0:T(2,128)S(1)} %copy-done.2, f32[48,64]{1,0:T(8,128)S(1)} %copy-done.1), custom_call_target="tpu_custom_call" | custom-call | tf_op jit(solution)/shard_map/pallas_call | solution.py:271
  165.2 0.6 copy.7
Async XLA Ops:
  6.5 71.6 %all-gather.2.cloned.1.call-start = ((), (), s32[]{:S(2)}) async-start(), calls=%async_computation | async-start | bytes 8650752 | tf_op jit(solution)/shard_map/all_gather | solution.py:269
  78.2 0.9 copy-start
  79.1 0.7 copy-start.1
  79.9 0.7 copy-start.2
  80.5 0.7 copy-start.3
Sparse Core Ops, SparseCore 0:
  10.5 67.6 all-gather.1

commit v2 on v1

--- a/solution.py
+++ b/solution.py
@@ -17,6 +17,32 @@
 TILE = 512
 MESH = pl.DeviceIdType.MESH
 
+SIDE = 4
+ACROSS = (0, -1, 1)
+PIECES = (
+    [(-1, 0, None), (1, 0, None), (2, 0, 0), (2, 0, 1)]
+    + [(step, -1, None) for step in ACROSS] + [(2, -1, 0), (2, -1, 1)]
+    + [(step, 1, None) for step in ACROSS] + [(2, 1, 0), (2, 1, 1)]
+    + [(step, 2, 0) for step in ACROSS + (2,)] + [(step, 2, 1) for step in ACROSS + (2,)]
+)
+OWN = len(PIECES)
+FORE, BACK, UP, DOWN = (1, 0), (-1, 0), (0, 1), (0, -1)
+OWN_TO = [(FORE, 0), (BACK, 1), (UP, 4), (DOWN, 9)]
+FORWARD = [
+    [(0, FORE, 2), (None, UP, 5), (None, DOWN, 10)],
+    [(1, BACK, 3), (None, UP, 6), (None, DOWN, 11)],
+    [(None, UP, 7), (None, DOWN, 12)],
+    [(None, UP, 8), (None, DOWN, 13)],
+    [(0, UP, 14)], [(0, UP, 15)], [(0, UP, 16)], [(None, UP, 17)], [],
+    [(1, DOWN, 18)], [(1, DOWN, 19)], [(1, DOWN, 20)], [], [(None, DOWN, 21)],
+] + [[]] * 8
+STAGES = [
+    ([0, 1, 4, 9], [(0, 0)]),
+    ([2, 3, 5, 10, 6, 11], [(-1, 0), (1, 0), (0, -1), (0, 1)]),
+    ([7, 12, 8, 13, 14, 18], [(-1, -1), (-1, 1), (1, -1), (1, 1), (2, 0), (0, 2)]),
+    ([15, 19, 16, 20, 17, 21], [(2, -1), (2, 1), (-1, 2), (1, 2), (2, 2)]),
+]
+
 
 def pick(index, values):
     result = values[-1]
@@ -27,9 +53,10 @@
 
 def kernel(
     chans, sectors,
-    full_ref, rows_ref, pot_ref, quanta_ref, start_ref, out_ref,
-    basis, flipped, state, rounded, weighted, turned,
-    whole, message, terms, table, level_send, level_recv, wave_send, wave_recv, hop_send, hop_recv, load_sem,
+    mine_ref, rows_ref, pot_ref, quanta_ref, start_ref, out_ref,
+    basis, flipped, state, rounded, weighted, summed, turned,
+    whole, message, terms, table, level_send, level_recv, wave_send, wave_recv, hop_send, hop_recv,
+    ring_send, ring_recv, twin_send, twin_recv,
 ):
     n = basis.shape[0]
     width = n // chans
@@ -50,9 +77,6 @@
     sends = jnp.logical_and(sector == last, following > 0)
     previous = first - 1
 
-    load = pltpu.make_async_copy(full_ref, basis, load_sem)
-    load.start()
-
     barrier = pltpu.get_barrier_semaphore()
 
     def greet(distance, carry):
@@ -117,6 +141,62 @@
 
         lax.fori_loop(1, chans, go, 0)
 
+    core, y_at, x_at = lax.rem(me, 2), lax.rem(me // 2, SIDE), me // (2 * SIDE)
+    twin = me + 1 - 2 * core
+    cut = n // 2
+
+    def chip_of(half, first_step, second_step):
+        dx, dy = (first_step, second_step) if half == 0 else (second_step, first_step)
+        return lax.rem(x_at + dx + SIDE, SIDE) * SIDE + lax.rem(y_at + dy + SIDE, SIDE)
+
+    def piece(half, owner, part):
+        begin, size = (0, width) if part is None else (part * (width // 2), width // 2)
+        rows = pl.ds(pl.multiple_of(owner * width + begin, width // 2), size)
+        return basis.at[rows, pl.ds(half * cut, cut)]
+
+    def ring_copy(half, first_step, second_step, part, toward, slot, source=None):
+        owner = chip_of(half, first_step, second_step) * 2 + core
+        return pltpu.make_async_remote_copy(
+            src_ref=piece(half, owner, part) if source is None else source,
+            dst_ref=piece(half, owner, part),
+            send_sem=ring_send.at[half, slot], recv_sem=ring_recv.at[half, slot],
+            device_id=(sector, chip_of(half, *toward) * 2 + core), device_id_type=MESH,
+        )
+
+    def twin_copy(half, slot, owner):
+        part = PIECES[slot][2]
+        return pltpu.make_async_remote_copy(
+            src_ref=piece(half, owner, part), dst_ref=piece(half, owner, part),
+            send_sem=twin_send.at[half, slot], recv_sem=twin_recv.at[half, slot],
+            device_id=(sector, twin), device_id_type=MESH,
+        )
+
+    def arrived(half, slot):
+        first_step, second_step, part = PIECES[slot]
+        ring_copy(half, first_step, second_step, part, (0, 1), slot).wait_recv()
+        for cut_to, toward, target in FORWARD[slot]:
+            ring_copy(half, first_step, second_step, part if cut_to is None else cut_to, toward, target).start()
+        twin_copy(half, slot, chip_of(half, first_step, second_step) * 2 + core).start()
+
+    def twin_arrived(half, slot):
+        first_step, second_step, _ = PIECES[slot]
+        twin_copy(half, slot, chip_of(half, first_step, second_step) * 2 + 1 - core).wait_recv()
+
+    def own_twin_copy(owner):
+        place = basis.at[pl.ds(pl.multiple_of(owner * width, width), width), :]
+        return pltpu.make_async_remote_copy(
+            src_ref=mine_ref, dst_ref=place, send_sem=twin_send.at[0, OWN], recv_sem=twin_recv.at[0, OWN],
+            device_id=(sector, twin), device_id_type=MESH,
+        )
+
+    for half in (0, 1):
+        for toward, target in OWN_TO:
+            ring_copy(
+                half, 0, 0, None, toward, target, mine_ref.at[:, pl.ds(half * cut, cut)]
+            ).start()
+    own_twin_copy(me).start()
+    basis[pl.ds(pl.multiple_of(me * width, width), width), :] = mine_ref[...]
+
     to_peers(level_copy)
 
     @pl.when(first == 0)
@@ -127,16 +207,34 @@
         )
         to_peers(wave_copy)
 
-    load.wait()
-
-    @pl.loop(0, n // 128)
-    def _(block):
-        rows = pl.ds(pl.multiple_of(block * 128, 128), 128)
-
-        @pl.loop(0, n // TILE)
-        def _(tile):
-            columns = pl.ds(pl.multiple_of(tile * TILE, TILE), TILE)
-            flipped[columns, rows] = jnp.transpose(basis[rows, columns])
+    top = 2 * sector + 1
+    bottom = 2 * first
+    top_row = rows_ref[top]
+    weighted[pl.ds(0, width), :] = (
+        mine_ref[...].astype(jnp.float32) * pot_ref[pl.ds(top_row, 1), :]
+    ).astype(jnp.bfloat16)
+    summed[...] = jnp.zeros_like(summed)
+
+    def factor_of(point, columns, size):
+        radius = jnp.full((1, size), radius_first, jnp.float32) + radius_step * point.astype(jnp.float32)
+        return table[0:1, columns] + table[1:2, columns] * (1.0 / (radius * radius))
+
+    def take(chip):
+        columns = pl.ds(pl.multiple_of(chip * 128, 128), 128)
+        for begin in range(0, n, TILE):
+            flipped[pl.ds(begin, TILE), columns] = jnp.transpose(basis[columns, pl.ds(begin, TILE)])
+        product = jnp.dot(weighted[pl.ds(0, width), :], flipped[:, columns], preferred_element_type=jnp.float32)
+        row = lax.broadcasted_iota(jnp.int32, (width, 128), 0)
+        column = lax.broadcasted_iota(jnp.int32, (width, 128), 1) + chip * 128
+        own = jnp.where(column == me * width + row, 1.0, 0.0)
+        new = factor_of(top, columns, 128) * own - step_square * product
+        both = jnp.concatenate([new, own], axis=0)
+        state[0, :, columns] = jnp.concatenate([own, jnp.zeros_like(own)], axis=0)
+        state[1, :, columns] = both
+        both = both.astype(jnp.bfloat16)
+        for begin in range(0, n, TILE):
+            tile = pl.ds(begin, TILE)
+            summed[:, tile] += jnp.dot(both, basis[columns, tile], preferred_element_type=jnp.float32)
 
     def level_wait(distance, carry):
         owner = lax.rem(me + distance, chans)
@@ -147,55 +245,62 @@
         ).wait_recv()
         return carry
 
-    lax.fori_loop(1, chans, level_wait, 0)
-
-    @pl.loop(0, chans // 2)
-    def _(pair):
-        table[:, pl.ds(pl.multiple_of(pair * 128, 128), 128)] = terms[2 * pair] + terms[2 * pair + 1]
-
-    top = 2 * sector + 1
-    bottom = 2 * first
-
-    @pl.loop(0, n // TILE)
-    def _(tile):
-        columns = pl.ds(pl.multiple_of(tile * TILE, TILE), TILE)
-        shape = (2 * width, TILE)
-        row = lax.broadcasted_iota(jnp.int32, shape, 0)
-        column = lax.broadcasted_iota(jnp.int32, shape, 1) + tile * TILE
-        later = row < width
-        own = column == me * width + jnp.where(later, row, row - width)
-        now = jnp.where(jnp.logical_and(own, later), 1.0, 0.0)
-        state[0, :, columns] = now
-        state[1, :, columns] = jnp.where(jnp.logical_and(own, jnp.logical_not(later)), -1.0, 0.0)
-        rounded[:, columns] = now.astype(jnp.bfloat16)
+    for stage, (slots, offsets) in enumerate(STAGES):
+        for slot in slots:
+            for half in (0, 1):
+                arrived(half, slot)
+        if stage == 0:
+            lax.fori_loop(1, chans, level_wait, 0)
+
+            @pl.loop(0, chans // 2)
+            def _(pair):
+                table[:, pl.ds(pl.multiple_of(pair * 128, 128), 128)] = terms[2 * pair] + terms[2 * pair + 1]
+
+            own_twin_copy(twin).wait_recv()
+        for slot in slots:
+            for half in (0, 1):
+                twin_arrived(half, slot)
+
+        def each(index, carry, offsets=offsets):
+            dx, dy = pick(index, [o[0] for o in offsets]), pick(index, [o[1] for o in offsets])
+            take(chip_of(0, dx, dy))
+            return carry
+
+        lax.fori_loop(0, len(offsets), each, 0)
+
+    steps = top - bottom + 1
+
+    def weigh(product, point, columns):
+        weighted[:, columns] = (product * pot_ref[pl.ds(rows_ref[point], 1), columns]).astype(jnp.bfloat16)
+
+    for begin in range(0, n, TILE):
+        weigh(summed[:, pl.ds(begin, TILE)], top - 1, pl.ds(begin, TILE))
 
     def back(step, carry):
         point = top - step
         current, other = lax.rem(step, 2), 1 - lax.rem(step, 2)
-        row = rows_ref[point]
-
-        @pl.loop(0, n // TILE)
-        def _(tile):
-            columns = pl.ds(pl.multiple_of(tile * TILE, TILE), TILE)
-            product = jnp.dot(rounded[...], basis[:, columns], preferred_element_type=jnp.float32)
-            weighted[:, columns] = (product * pot_ref[pl.ds(row, 1), columns]).astype(jnp.bfloat16)
-
-        radius = jnp.full((1, TILE), radius_first, jnp.float32) + radius_step * point.astype(jnp.float32)
-        inverse = 1.0 / (radius * radius)
-
-        @pl.loop(0, n // TILE)
-        def _(tile):
-            columns = pl.ds(pl.multiple_of(tile * TILE, TILE), TILE)
+        for begin in range(0, n, TILE):
+            columns = pl.ds(begin, TILE)
             product = jnp.dot(weighted[...], flipped[:, columns], preferred_element_type=jnp.float32)
-            factor = table[0:1, columns] + table[1:2, columns] * inverse
-            new = factor * state[current, :, columns] - state[other, :, columns] - step_square * product
+            new = (
+                factor_of(point, columns, TILE) * state[current, :, columns]
+                - state[other, :, columns] - step_square * product
+            )
             state[other, :, columns] = new
             rounded[:, columns] = new.astype(jnp.bfloat16)
 
+        @pl.when(step + 1 < steps)
+        def _():
+            for begin in range(0, n, TILE):
+                columns = pl.ds(begin, TILE)
+                weigh(
+                    jnp.dot(rounded[...], basis[:, columns], preferred_element_type=jnp.float32),
+                    point - 1, columns,
+                )
+
         return carry
 
-    steps = top - bottom + 1
-    lax.fori_loop(0, steps, back, 0)
+    lax.fori_loop(1, steps, back, 0)
     newest, older = lax.rem(steps, 2), 1 - lax.rem(steps, 2)
 
     low = lax.broadcasted_iota(jnp.int32, (2 * width, 128), 1) < width
@@ -260,19 +365,26 @@
     out_ref[1] = result[:, :width]
     sent_to_peers(level_copy)
     sent_to_peers(wave_copy)
+    for half in (0, 1):
+        for toward, target in OWN_TO:
+            ring_copy(half, 0, 0, None, toward, target).wait_send()
+        for slot, (first_step, second_step, part) in enumerate(PIECES):
+            for cut_to, toward, target in FORWARD[slot]:
+                ring_copy(half, first_step, second_step, part if cut_to is None else cut_to, toward, target).wait_send()
+            twin_copy(half, slot, me).wait_send()
+    own_twin_copy(me).wait_send()
 
 
 def local(angular, potential, point_rows, quanta, start_waves):
     chans, sectors = lax.axis_size("chan"), lax.axis_size("sector")
     points, n = angular.shape[0], angular.shape[1] * chans
     solutions, width = start_waves.shape
-    full = lax.all_gather(angular.T, "chan", axis=0, tiled=True)
     vmem = pl.BlockSpec(memory_space=pltpu.VMEM)
     return pl.pallas_call(
         functools.partial(kernel, chans, sectors),
         out_shape=jax.ShapeDtypeStruct((2, solutions, width), jnp.float32),
         in_specs=[
-            pl.BlockSpec(memory_space=pl.ANY),
+            vmem,
             pl.BlockSpec(memory_space=pltpu.SMEM),
             vmem, vmem, vmem,
         ],
@@ -283,6 +395,7 @@
             pltpu.VMEM((2, 2 * width, n), jnp.float32),
             pltpu.VMEM((2 * width, n), jnp.bfloat16),
             pltpu.VMEM((2 * width, points), jnp.bfloat16),
+            pltpu.VMEM((2 * width, points), jnp.float32),
             pltpu.VMEM((2 * n, 2 * width), jnp.bfloat16),
             pltpu.VMEM((solutions, 2 * n), jnp.bfloat16),
             pltpu.VMEM((solutions, 2 * width), jnp.bfloat16),
@@ -294,12 +407,15 @@
             pltpu.SemaphoreType.DMA((chans,)),
             pltpu.SemaphoreType.DMA((max(GROUPS),)),
             pltpu.SemaphoreType.DMA,
-            pltpu.SemaphoreType.DMA,
+            pltpu.SemaphoreType.DMA((2, OWN)),
+            pltpu.SemaphoreType.DMA((2, OWN)),
+            pltpu.SemaphoreType.DMA((2, OWN + 1)),
+            pltpu.SemaphoreType.DMA((2, OWN + 1)),
         ],
         compiler_params=pltpu.CompilerParams(
             collective_id=0, has_side_effects=True, vmem_limit_bytes=48 * 1024 * 1024
         ),
-    )(full, point_rows, potential, quanta, start_waves)
+    )(angular.T, point_rows, potential, quanta, start_waves)
 
 
 def solution(mesh):

time: 173 us -> 107 us (0.62)
  waiting for transfers between devices: 71.6 us -> 0 us
  Pallas kernels: 84 us -> 103 us
  between operations: 13.4 us -> 0.01 us
    all_gather x1 -> x0, waiting for transfers between devices: 70.9 us -> none  [local(): full = lax.all_gather(angular.T, 'chan', axis=0, tiled=True)]
    pallas_call x1, Pallas kernels: 84 us -> 103 us  [local(): pl.pallas_call(functools.partial(kernel, chans, sectors), out_shape=jax.S...]
    unnamed x9 -> x11, local copies, waits for them, and re-layouts: 3.64 us -> 3.94 us
  transfers between devices with their start and end apart: 1 -> 0, of which waited for: 1 -> 0; matrix products, arithmetic and copies ran while one was open for 0% -> 0% of each run, Pallas kernels for 0% -> 0%
where the time goes in v2:
time: 107 us
  Pallas kernels  103 us (96%)
  local copies, waits for them, and re-layouts  3.94 us (4%)
    pallas_call x1, Pallas kernels, local(): pl.pallas_call(functools.partial(kernel, chans, sectors), out_shape=jax.S...  103 us
    unnamed x11, local copies, waits for them, and re-layouts  3.94 us

profile of v2, /device:TPU:481, one launch (start us, length us, event | category | flops | bytes accessed | tf_op | source)
XLA Modules:
  0.0 106.9 jit_solution(13153499360907484557)
XLA Ops:
  0.0 0.0 copy-start.3
  0.0 0.0 copy-start.4
  0.0 0.7 copy-done.3
  0.7 0.0 copy-done.4
  0.7 0.0 copy-start
  0.7 0.9 copy-done
  1.6 0.0 copy-start.1
  1.6 0.9 copy-done.1
  2.6 0.0 copy-start.2
  2.6 0.7 copy-done.2
  3.3 103.0 %shard_map.55 = f32[2,48,64]{2,1,0:T(8,128)S(1)} custom-call(bf16[64,2048]{1,0:T(8,128)(2,1)S(1)} %bitcast.1, s32[32]{0:T(128)S(1)} %copy-done.4, f32[32,2048]{1,0:T(8,128)S(1)} %copy-done.1, s32[2,64]{1,0:T(2,128)S(1)} %copy-done.3, f32[48,64]{1,0:T(8,128)S(1)} %copy-done.2), custom_call_target="tpu_custom_call" | custom-call | tf_op jit(solution)/shard_map/pallas_call | solution.py:383
  106.3 0.6 copy.7
Async XLA Ops:
  0.0 0.7 copy-start.3
  0.0 0.7 copy-start.4
  0.7 1.0 copy-start
  1.6 0.9 copy-start.1
  2.6 0.7 copy-start.2

commit v3 on v2

v3 whole, which is shorter than its diff:
```python
import functools

import jax
import jax.numpy as jnp
from jax import lax
from jax.experimental import pallas as pl
from jax.experimental.pallas import tpu as pltpu
from jax.sharding import PartitionSpec as P

energy = 3.5
rotor_const = 0.02
radius_first = 8.0
radius_step = 0.5
step_square = 0.08

GROUPS = (3, 5, 8)
PASS_AT = (99, 8, 12)
TILE = 512
MESH = pl.DeviceIdType.MESH

SIDE = 4
STEPS = (0, -1, 1, 2)
PIECES = [(f, s, part) for f in STEPS for s in STEPS if (f, s) != (0, 0) for part in (0, 1)]
OWN = len(PIECES)
FORE, BACK, UP, DOWN = (1, 0), (-1, 0), (0, 1), (0, -1)
OWN_TO = [
    (part, toward, PIECES.index((-toward[0], -toward[1], part)))
    for turn in (0, 1)
    for toward, early in ((FORE, 0), (BACK, 1), (UP, 0), (DOWN, 1))
    for part in (early if turn == 0 else 1 - early,)
]


def sent_on(piece):
    f, s, part = piece
    result = []
    if s == 0:
        if (f, part) == (-1, 0):
            result.append((FORE, PIECES.index((2, 0, 0))))
        if (f, part) == (1, 1):
            result.append((BACK, PIECES.index((2, 0, 1))))
        result += [(UP, PIECES.index((f, -1, part))), (DOWN, PIECES.index((f, 1, part)))]
    if (s, part) == (-1, 0):
        result.append((UP, PIECES.index((f, 2, 0))))
    if (s, part) == (1, 1):
        result.append((DOWN, PIECES.index((f, 2, 1))))
    return result


FORWARD = [sent_on(piece) for piece in PIECES]
FAR_FIRST = sorted(
    [(dx, dy) for dx in STEPS for dy in STEPS if (dx, dy) != (0, 0)], key=lambda o: -abs(o[0]) - abs(o[1])
)
ORDER = [
    ("pieces", [(-1, 0, 0), (1, 0, 1), (0, -1, 0), (0, 1, 1), (-1, 0, 1), (1, 0, 0), (0, -1, 1), (0, 1, 0)]),
    ("levels", 0), ("take", [(0, 0)]),
    ("pieces", [(2, 0, 0), (2, 0, 1), (-1, -1, 0), (1, -1, 0), (-1, 1, 1), (1, 1, 1)]),
    ("levels", 1), ("take", [(-1, 0), (0, -1)]),
    ("pieces", [(0, 2, 0), (0, 2, 1), (-1, -1, 1), (1, -1, 1), (-1, 1, 0), (1, 1, 0)]),
    ("take", [(1, 0), (0, 1)]),
    ("pieces", [(2, -1, 0), (2, 1, 1)]), ("take", [(-1, -1), (1, -1)]),
    ("pieces", [(2, -1, 1), (2, 1, 0)]), ("take", [(-1, 1), (1, 1)]),
    ("pieces", [(-1, 2, 0), (-1, 2, 1)]), ("take", [(2, 0), (0, 2)]),
    ("pieces", [(1, 2, 0), (1, 2, 1)]), ("take", [(2, -1), (-1, 2)]),
    ("waves", 0), ("waves", 1), ("take", [(2, 1), (1, 2)]), ("pieces", [(2, 2, 0), (2, 2, 1)]), ("take", [(2, 2)]),
]


def pick(index, values):
    result = values[-1]
    for place in range(len(values) - 1):
        result = jnp.where(index == place, values[place], result)
    return result


def kernel(
    chans, sectors,
    mine_ref, rows_ref, pot_in, quanta_in, start_in, out_ref,
    pot_ref, quanta_ref, start_ref,
    basis, flipped, state, rounded, weighted, summed, turned,
    whole, message, terms, table, level_send, level_recv, wave_send, wave_recv, hop_send, hop_recv,
    ring_send, ring_recv, twin_send, twin_recv, load_sem,
):
    n = basis.shape[0]
    width = n // chans
    sector, me = lax.axis_index("sector"), lax.axis_index("chan")
    first_of, last_of, next_of, pass_of = [], [], [], []
    start = 0
    for index, size in enumerate(GROUPS):
        following = GROUPS[index + 1] if index + 1 < len(GROUPS) else 0
        for _ in range(size):
            first_of.append(start)
            last_of.append(start + size - 1)
            next_of.append(following)
            pass_of.append(PASS_AT[index])
        start += size
    first = pick(sector, first_of)
    last = pick(sector, last_of)
    following = pick(sector, next_of)
    pass_at = pick(sector, pass_of)
    sends = jnp.logical_and(sector == last, following > 0)
    previous = first - 1

    core, y_at, x_at = lax.rem(me, 2), lax.rem(me // 2, SIDE), me // (2 * SIDE)
    twin = me + 1 - 2 * core
    cut = n // 2
    own_rows = pl.ds(pl.multiple_of(me * width, width), width)
    loads = [
        pltpu.make_async_copy(source, place, load_sem.at[index])
        for index, (source, place) in enumerate([
            (quanta_in, quanta_ref), (start_in, start_ref), (mine_ref, basis.at[own_rows, :]), (pot_in, pot_ref),
        ])
    ]
    for load in loads:
        load.start()

    barrier = pltpu.get_barrier_semaphore()

    def greet(distance, carry):
        peer = lax.rem(me + distance, chans)
        pl.semaphore_signal(barrier, inc=1, device_id=(sector, peer), device_id_type=MESH)
        return carry

    lax.fori_loop(1, chans, greet, 0)

    @pl.when(sends)
    def _():
        def greet_next(step, carry):
            pl.semaphore_signal(barrier, inc=1, device_id=(sector + 1 + step, me), device_id_type=MESH)
            return carry

        lax.fori_loop(0, following, greet_next, 0)

    @pl.when(first > 0)
    def _():
        pl.semaphore_signal(barrier, inc=1, device_id=(previous, me), device_id_type=MESH)

    greeted = chans - 1 + jnp.where(sends, following, 0) + jnp.where(first > 0, 1, 0)
    pl.semaphore_wait(barrier, greeted)

    def level_copy(peer):
        return pltpu.make_async_remote_copy(
            src_ref=terms.at[me], dst_ref=terms.at[me],
            send_sem=level_send.at[peer], recv_sem=level_recv.at[me],
            device_id=(sector, peer), device_id_type=MESH,
        )

    def wave_slot(owner):
        return whole.at[:, pl.ds(pl.multiple_of(owner * 2 * width, 2 * width), 2 * width)]

    def wave_copy(peer):
        return pltpu.make_async_remote_copy(
            src_ref=wave_slot(me), dst_ref=wave_slot(me),
            send_sem=wave_send.at[peer], recv_sem=wave_recv.at[me],
            device_id=(sector, peer), device_id_type=MESH,
        )

    def to_peers(make, portion=None):
        for place, (dx, dy) in enumerate(FAR_FIRST):
            if portion in (None, place % 2):
                for side in (0, 1):
                    make(chip_of(0, dx, dy) * 2 + side).start()
        if portion != 0:
            make(twin).start()

    def sent_to_peers(make):
        def go(distance, carry):
            make(lax.rem(me + distance, chans)).wait_send()
            return carry

        lax.fori_loop(1, chans, go, 0)

    def chip_of(half, first_step, second_step):
        dx, dy = (first_step, second_step) if half == 0 else (second_step, first_step)
        return lax.rem(x_at + dx + SIDE, SIDE) * SIDE + lax.rem(y_at + dy + SIDE, SIDE)

    def piece(half, owner, part):
        begin, size = (0, width) if part is None else (part * (width // 2), width // 2)
        rows = pl.ds(pl.multiple_of(owner * width + begin, width // 2), size)
        return basis.at[rows, pl.ds(half * cut, cut)]

    def ring_copy(half, slot, toward, target, source=None):
        first_step, second_step, part = (0, 0, PIECES[target][2]) if slot is None else PIECES[slot]
        owner = chip_of(half, first_step, second_step) * 2 + core
        return pltpu.make_async_remote_copy(
            src_ref=piece(half, owner, part) if source is None else source,
            dst_ref=piece(half, owner, part),
            send_sem=ring_send.at[half, target], recv_sem=ring_recv.at[half, target],
            device_id=(sector, chip_of(half, *toward) * 2 + core), device_id_type=MESH,
        )

    def twin_copy(half, slot, side):
        first_step, second_step, _ = PIECES[slot]
        place = piece(half, chip_of(half, first_step, second_step) * 2 + side, None)
        return pltpu.make_async_remote_copy(
            src_ref=place, dst_ref=place,
            send_sem=twin_send.at[half, slot // 2], recv_sem=twin_recv.at[half, slot // 2],
            device_id=(sector, twin), device_id_type=MESH,
        )

    def arrived(half, slot, both):
        pltpu.make_async_remote_copy(
            src_ref=mine_ref.at[pl.ds(0, width // 2), pl.ds(0, cut)], dst_ref=piece(
                half, chip_of(half, *PIECES[slot][:2]) * 2 + core, PIECES[slot][2]
            ),
            send_sem=ring_send.at[half, slot], recv_sem=ring_recv.at[half, slot],
            device_id=(sector, twin), device_id_type=MESH,
        ).wait_recv()
        for toward, target in FORWARD[slot]:
            ring_copy(half, slot, toward, target).start()
        if both:
            twin_copy(half, slot, core).start()

    def own_twin_copy(owner):
        place = basis.at[pl.ds(pl.multiple_of(owner * width, width), width), :]
        return pltpu.make_async_remote_copy(
            src_ref=mine_ref, dst_ref=place, send_sem=twin_send.at[0, OWN // 2], recv_sem=twin_recv.at[0, OWN // 2],
            device_id=(sector, twin), device_id_type=MESH,
        )

    def own_part(half, part):
        return mine_ref.at[pl.ds(part * (width // 2), width // 2), pl.ds(half * cut, cut)]

    for part, toward, target in OWN_TO:
        for half in (0, 1):
            ring_copy(half, None, toward, target, own_part(half, part)).start()
    own_twin_copy(me).start()

    loads[0].wait()
    quanta = quanta_ref[...].astype(jnp.float32)
    j_values, l_values = quanta[0:1, :], quanta[1:2, :]
    a_row = 2.0 - step_square * (energy - rotor_const * j_values * (j_values + 1.0))
    b_row = step_square * (l_values * (l_values + 1.0))
    ab = jnp.concatenate([a_row, b_row, jnp.zeros((6, width), jnp.float32)], axis=0)
    lane = lax.broadcasted_iota(jnp.int32, (8, 2 * width), 1)
    half = lane // width
    terms[me] = jnp.where(half == lax.rem(me, 2), jnp.concatenate([ab, ab], axis=1), 0.0)
    loads[1].wait()

    @pl.when(first == 0)
    def _():
        waves = start_ref[...].astype(jnp.bfloat16)
        whole[:, pl.ds(pl.multiple_of(me * 2 * width, 2 * width), 2 * width)] = jnp.concatenate(
            [waves, waves], axis=1
        )

    top = 2 * sector + 1
    bottom = 2 * first
    top_row = rows_ref[top]
    loads[2].wait()
    loads[3].wait()
    weighted[pl.ds(0, width), :] = (
        basis[own_rows, :].astype(jnp.float32) * pot_ref[pl.ds(top_row, 1), :]
    ).astype(jnp.bfloat16)
    summed[...] = jnp.zeros_like(summed)

    def level_of(point, a_row, b_row):
        radius = jnp.full(a_row.shape, radius_first, jnp.float32) + radius_step * point.astype(jnp.float32)
        return a_row + b_row * (1.0 / (radius * radius))

    own_level = level_of(top, terms[me, 0:1, :], terms[me, 1:2, :])

    def take(chips):
        places, news = [], []
        for chip in chips:
            columns = pl.ds(pl.multiple_of(chip * 128, 128), 128)
            for begin in range(0, n, TILE):
                flipped[pl.ds(begin, TILE), columns] = jnp.transpose(basis[columns, pl.ds(begin, TILE)])
            places.append(columns)
        for chip, columns in zip(chips, places):
            product = jnp.dot(
                weighted[pl.ds(0, width), :], flipped[:, columns], preferred_element_type=jnp.float32
            )
            row = lax.broadcasted_iota(jnp.int32, (width, 128), 0)
            column = lax.broadcasted_iota(jnp.int32, (width, 128), 1) + chip * 128
            own = jnp.where(column == me * width + row, 1.0, 0.0)
            both = jnp.concatenate([own_level * own - step_square * product, own], axis=0)
            state[0, :, columns] = jnp.concatenate([own, jnp.zeros_like(own)], axis=0)
            state[1, :, columns] = both
            news.append(both.astype(jnp.bfloat16))
        for begin in range(0, n, TILE):
            tile = pl.ds(begin, TILE)
            total = summed[:, tile]
            for columns, both in zip(places, news):
                total += jnp.dot(both, basis[columns, tile], preferred_element_type=jnp.float32)
            summed[:, tile] = total

    def level_wait(distance, carry):
        owner = lax.rem(me + distance, chans)
        pltpu.make_async_remote_copy(
            src_ref=terms.at[owner], dst_ref=terms.at[owner],
            send_sem=level_send.at[owner], recv_sem=level_recv.at[owner],
            device_id=(sector, owner), device_id_type=MESH,
        ).wait_recv()
        return carry

    handed = ([], [])
    for kind, what in ORDER:
        if kind == "pieces":
            for name in what:
                for half in (0, 1):
                    handed[half].append(name)
                    arrived(half, PIECES.index(name), name[:2] + (1 - name[2],) in handed[half])
        elif kind == "levels":
            to_peers(level_copy, what)
        elif kind == "waves":
            @pl.when(first == 0)
            def _(portion=what):
                to_peers(wave_copy, portion)
        else:
            for dx, dy in what:
                if (dx, dy) == (0, 0):
                    own_twin_copy(twin).wait_recv()
                else:
                    for half, steps_to in ((0, (dx, dy)), (1, (dy, dx))):
                        twin_copy(half, PIECES.index(steps_to + (0,)), 1 - core).wait_recv()
            take([chip_of(0, dx, dy) for dx, dy in what])

    lax.fori_loop(1, chans, level_wait, 0)

    @pl.loop(0, chans // 2)
    def _(pair):
        table[:, pl.ds(pl.multiple_of(pair * 128, 128), 128)] = terms[2 * pair] + terms[2 * pair + 1]

    steps = top - bottom + 1

    def weigh(product, point, columns):
        weighted[:, columns] = (product * pot_ref[pl.ds(rows_ref[point], 1), columns]).astype(jnp.bfloat16)

    for begin in range(0, n, TILE):
        weigh(summed[:, pl.ds(begin, TILE)], top - 1, pl.ds(begin, TILE))

    def pass_on():
        pltpu.make_async_remote_copy(
            src_ref=message, dst_ref=wave_slot(me), send_sem=hop_send.at[0], recv_sem=hop_recv,
            device_id=(previous, me), device_id_type=MESH,
        ).wait_recv()
        to_peers(wave_copy)

    def back(step, carry):
        point = top - step

        @pl.when(jnp.logical_and(step == pass_at, first > 0))
        def _():
            pass_on()

        current, other = lax.rem(step, 2), 1 - lax.rem(step, 2)
        for begin in range(0, n, TILE):
            columns = pl.ds(begin, TILE)
            product = jnp.dot(weighted[...], flipped[:, columns], preferred_element_type=jnp.float32)
            new = (
                level_of(point, table[0:1, columns], table[1:2, columns]) * state[current, :, columns]
                - state[other, :, columns] - step_square * product
            )
            state[other, :, columns] = new
            rounded[:, columns] = new.astype(jnp.bfloat16)

        @pl.when(step + 1 < steps)
        def _():
            for begin in range(0, n, TILE):
                columns = pl.ds(begin, TILE)
                weigh(
                    jnp.dot(rounded[...], basis[:, columns], preferred_element_type=jnp.float32),
                    point - 1, columns,
                )

        return carry

    lax.fori_loop(1, steps, back, 0)

    @pl.when(jnp.logical_and(steps <= pass_at, first > 0))
    def _():
        pass_on()

    newest, older = lax.rem(steps, 2), 1 - lax.rem(steps, 2)

    def differences(rows):
        return jnp.concatenate([rows[:width], rows[:width] - rows[width:]], axis=0)

    @pl.loop(0, chans // 4)
    def _(quarter):
        for part in range(2):
            pair = 2 * quarter + part
            columns = pl.ds(pl.multiple_of(pair * 128, 128), 128)
            before = differences(state[older, :, columns])
            main = differences(state[newest, :, columns]) - before
            main, before = (jnp.transpose(v.astype(jnp.bfloat16)) for v in (main, before))
            for side in range(2):
                place = pl.ds(pl.multiple_of((2 * pair + side) * 128, 128), 128)
                lines = slice(side * width, (side + 1) * width)
                turned[place, :] = jnp.concatenate([main[lines], before[lines]], axis=0)

    def wave_wait(distance, carry):
        owner = lax.rem(me + distance, chans)
        pltpu.make_async_remote_copy(
            src_ref=wave_slot(owner), dst_ref=wave_slot(owner),
            send_sem=wave_send.at[owner], recv_sem=wave_recv.at[owner],
            device_id=(sector, owner), device_id_type=MESH,
        ).wait_recv()
        return carry

    lax.fori_loop(1, chans, wave_wait, 0)
    result = jnp.dot(whole[...], turned[...], preferred_element_type=jnp.float32)
    swapped = pltpu.roll(result, width, 1)

    def hop_copy(step):
        return pltpu.make_async_remote_copy(
            src_ref=message, dst_ref=wave_slot(me), send_sem=hop_send.at[step], recv_sem=hop_recv,
            device_id=(sector + 1 + step, me), device_id_type=MESH,
        )

    @pl.when(sends)
    def _():
        message[...] = result.astype(jnp.bfloat16)

        def go(step, carry):
            hop_copy(following - 1 - step).start()
            return carry

        lax.fori_loop(0, following, go, 0)

        def done(step, carry):
            hop_copy(step).wait_send()
            return carry

        lax.fori_loop(0, following, done, 0)

    out_ref[0] = (result - swapped)[:, :width]
    out_ref[1] = result[:, :width]
    sent_to_peers(level_copy)
    sent_to_peers(wave_copy)
    for half in (0, 1):
        for part, toward, target in OWN_TO:
            ring_copy(half, None, toward, target, own_part(half, part)).wait_send()
        for slot in range(OWN):
            for toward, target in FORWARD[slot]:
                ring_copy(half, slot, toward, target).wait_send()
            if slot % 2 == 0:
                twin_copy(half, slot, core).wait_send()
    own_twin_copy(me).wait_send()


def local(angular, potential, point_rows, quanta, start_waves):
    chans, sectors = lax.axis_size("chan"), lax.axis_size("sector")
    points, n = angular.shape[0], angular.shape[1] * chans
    solutions, width = start_waves.shape
    vmem, hbm = pl.BlockSpec(memory_space=pltpu.VMEM), pl.BlockSpec(memory_space=pltpu.HBM)
    return pl.pallas_call(
        functools.partial(kernel, chans, sectors),
        out_shape=jax.ShapeDtypeStruct((2, solutions, width), jnp.float32),
        in_specs=[
            hbm,
            pl.BlockSpec(memory_space=pltpu.SMEM),
            hbm, hbm, hbm,
        ],
        out_specs=vmem,
        scratch_shapes=[
            pltpu.VMEM(potential.shape, jnp.float32),
            pltpu.VMEM(quanta.shape, jnp.int32),
            pltpu.VMEM(start_waves.shape, jnp.float32),
            pltpu.VMEM((n, points), jnp.bfloat16),
            pltpu.VMEM((points, n), jnp.bfloat16),
            pltpu.VMEM((2, 2 * width, n), jnp.float32),
            pltpu.VMEM((2 * width, n), jnp.bfloat16),
            pltpu.VMEM((2 * width, points), jnp.bfloat16),
            pltpu.VMEM((2 * width, points), jnp.float32),
            pltpu.VMEM((2 * n, 2 * width), jnp.bfloat16),
            pltpu.VMEM((solutions, 2 * n), jnp.bfloat16),
            pltpu.VMEM((solutions, 2 * width), jnp.bfloat16),
            pltpu.VMEM((chans, 8, 2 * width), jnp.float32),
            pltpu.VMEM((8, n), jnp.float32),
            pltpu.SemaphoreType.DMA((chans,)),
            pltpu.SemaphoreType.DMA((chans,)),
            pltpu.SemaphoreType.DMA((chans,)),
            pltpu.SemaphoreType.DMA((chans,)),
            pltpu.SemaphoreType.DMA((max(GROUPS),)),
            pltpu.SemaphoreType.DMA,
            pltpu.SemaphoreType.DMA((2, OWN)),
            pltpu.SemaphoreType.DMA((2, OWN)),
            pltpu.SemaphoreType.DMA((2, OWN // 2 + 1)),
            pltpu.SemaphoreType.DMA((2, OWN // 2 + 1)),
            pltpu.SemaphoreType.DMA((4,)),
        ],
        compiler_params=pltpu.CompilerParams(
            collective_id=0, has_side_effects=True, vmem_limit_bytes=60 * 1024 * 1024
        ),
    )(angular.T, point_rows, potential, quanta, start_waves)


def solution(mesh):
    placed = (P(None, "chan"), P(), P(), P(None, "chan"), P(None, "chan"))
    return jax.shard_map(
        local, mesh=mesh, in_specs=placed, out_specs=P("sector", None, "chan"), check_vma=False
    )
```

time: 107 us -> 91.2 us (0.85)
  Pallas kernels: 103 us -> 89.1 us
  local copies, waits for them, and re-layouts: 3.94 us -> 1.42 us
    pallas_call x1, Pallas kernels: 103 us -> 89.1 us  [local(): pl.pallas_call(functools.partial(kernel, chans, sectors), out_shape=jax.S...]
    unnamed x11 -> x1, local copies, waits for them, and re-layouts: 3.94 us -> 1.42 us
where the time goes in v3:
time: 91.2 us; the launch traced here: 90.5 us
  Pallas kernels  89.1 us (98%)
  local copies, waits for them, and re-layouts  1.42 us (2%)
    pallas_call x1, Pallas kernels, local(): pl.pallas_call(functools.partial(kernel, chans, sectors), out_shape=jax.S...  89.1 us

profile of v3, /device:TPU:481, one launch (start us, length us, event | category | flops | bytes accessed | tf_op | source)
XLA Modules:
  0.0 90.5 jit_solution(7474881557447997459)
XLA Ops:
  0.0 89.1 %shard_map.55 = f32[2,48,64]{2,1,0:T(8,128)} custom-call(bf16[64,2048]{1,0:T(8,128)(2,1)} %bitcast.1, s32[32]{0:T(128)} %rows_ref.1, f32[32,2048]{1,0:T(8,128)} %pot_in.1, s32[2,64]{1,0:T(2,128)} %quanta_in.1, f32[48,64]{1,0:T(8,128)} %start_in.1), custom_call_target="tpu_custom_call" | custom-call | tf_op jit(solution)/shard_map/pallas_call | solution.py:448
  89.1 1.4 %copy.7 = f32[2,48,64]{2,1,0:T(8,128)} copy(f32[2,48,64]{2,1,0:T(8,128)} %shard_map.55) | data formatting | bytes 49152

commit v4 on v3

--- a/solution.py
+++ b/solution.py
@@ -13,8 +13,8 @@
 radius_step = 0.5
 step_square = 0.08
 
-GROUPS = (3, 5, 8)
-PASS_AT = (99, 8, 12)
+GROUPS = (2, 3, 5, 6)
+PASS_AT = (99, 99, 99, 99)
 TILE = 512
 MESH = pl.DeviceIdType.MESH
 
@@ -141,7 +141,7 @@
     def level_copy(peer):
         return pltpu.make_async_remote_copy(
             src_ref=terms.at[me], dst_ref=terms.at[me],
-            send_sem=level_send.at[peer], recv_sem=level_recv.at[me],
+            send_sem=level_send, recv_sem=level_recv,
             device_id=(sector, peer), device_id_type=MESH,
         )
 
@@ -151,7 +151,7 @@
     def wave_copy(peer):
         return pltpu.make_async_remote_copy(
             src_ref=wave_slot(me), dst_ref=wave_slot(me),
-            send_sem=wave_send.at[peer], recv_sem=wave_recv.at[me],
+            send_sem=wave_send, recv_sem=wave_recv,
             device_id=(sector, peer), device_id_type=MESH,
         )
 
@@ -163,13 +163,6 @@
         if portion != 0:
             make(twin).start()
 
-    def sent_to_peers(make):
-        def go(distance, carry):
-            make(lax.rem(me + distance, chans)).wait_send()
-            return carry
-
-        lax.fori_loop(1, chans, go, 0)
-
     def chip_of(half, first_step, second_step):
         dx, dy = (first_step, second_step) if half == 0 else (second_step, first_step)
         return lax.rem(x_at + dx + SIDE, SIDE) * SIDE + lax.rem(y_at + dy + SIDE, SIDE)
@@ -185,7 +178,7 @@
         return pltpu.make_async_remote_copy(
             src_ref=piece(half, owner, part) if source is None else source,
             dst_ref=piece(half, owner, part),
-            send_sem=ring_send.at[half, target], recv_sem=ring_recv.at[half, target],
+            send_sem=ring_send, recv_sem=ring_recv.at[half, target],
             device_id=(sector, chip_of(half, *toward) * 2 + core), device_id_type=MESH,
         )
 
@@ -194,7 +187,7 @@
         place = piece(half, chip_of(half, first_step, second_step) * 2 + side, None)
         return pltpu.make_async_remote_copy(
             src_ref=place, dst_ref=place,
-            send_sem=twin_send.at[half, slot // 2], recv_sem=twin_recv.at[half, slot // 2],
+            send_sem=twin_send, recv_sem=twin_recv.at[half, slot // 2],
             device_id=(sector, twin), device_id_type=MESH,
         )
 
@@ -203,7 +196,7 @@
             src_ref=mine_ref.at[pl.ds(0, width // 2), pl.ds(0, cut)], dst_ref=piece(
                 half, chip_of(half, *PIECES[slot][:2]) * 2 + core, PIECES[slot][2]
             ),
-            send_sem=ring_send.at[half, slot], recv_sem=ring_recv.at[half, slot],
+            send_sem=ring_send, recv_sem=ring_recv.at[half, slot],
             device_id=(sector, twin), device_id_type=MESH,
         ).wait_recv()
         for toward, target in FORWARD[slot]:
@@ -214,7 +207,7 @@
     def own_twin_copy(owner):
         place = basis.at[pl.ds(pl.multiple_of(owner * width, width), width), :]
         return pltpu.make_async_remote_copy(
-            src_ref=mine_ref, dst_ref=place, send_sem=twin_send.at[0, OWN // 2], recv_sem=twin_recv.at[0, OWN // 2],
+            src_ref=mine_ref, dst_ref=place, send_sem=twin_send, recv_sem=twin_recv.at[0, OWN // 2],
             device_id=(sector, twin), device_id_type=MESH,
         )
 
@@ -285,15 +278,6 @@
                 total += jnp.dot(both, basis[columns, tile], preferred_element_type=jnp.float32)
             summed[:, tile] = total
 
-    def level_wait(distance, carry):
-        owner = lax.rem(me + distance, chans)
-        pltpu.make_async_remote_copy(
-            src_ref=terms.at[owner], dst_ref=terms.at[owner],
-            send_sem=level_send.at[owner], recv_sem=level_recv.at[owner],
-            device_id=(sector, owner), device_id_type=MESH,
-        ).wait_recv()
-        return carry
-
     handed = ([], [])
     for kind, what in ORDER:
         if kind == "pieces":
@@ -316,7 +300,14 @@
                         twin_copy(half, PIECES.index(steps_to + (0,)), 1 - core).wait_recv()
             take([chip_of(0, dx, dy) for dx, dy in what])
 
-    lax.fori_loop(1, chans, level_wait, 0)
+    def all_of(place, send_sem, recv_sem):
+        return pltpu.make_async_remote_copy(
+            src_ref=place, dst_ref=place, send_sem=send_sem, recv_sem=recv_sem,
+            device_id=(sector, twin), device_id_type=MESH,
+        )
+
+    levels = all_of(terms.at[pl.ds(0, chans - 1)], level_send, level_recv)
+    levels.wait_recv()
 
     @pl.loop(0, chans // 2)
     def _(pair):
@@ -390,16 +381,8 @@
                 lines = slice(side * width, (side + 1) * width)
                 turned[place, :] = jnp.concatenate([main[lines], before[lines]], axis=0)
 
-    def wave_wait(distance, carry):
-        owner = lax.rem(me + distance, chans)
-        pltpu.make_async_remote_copy(
-            src_ref=wave_slot(owner), dst_ref=wave_slot(owner),
-            send_sem=wave_send.at[owner], recv_sem=wave_recv.at[owner],
-            device_id=(sector, owner), device_id_type=MESH,
-        ).wait_recv()
-        return carry
-
-    lax.fori_loop(1, chans, wave_wait, 0)
+    waves = all_of(whole.at[:, pl.ds(0, (chans - 1) * 2 * width)], wave_send, wave_recv)
+    waves.wait_recv()
     result = jnp.dot(whole[...], turned[...], preferred_element_type=jnp.float32)
     swapped = pltpu.roll(result, width, 1)
 
@@ -427,17 +410,10 @@
 
     out_ref[0] = (result - swapped)[:, :width]
     out_ref[1] = result[:, :width]
-    sent_to_peers(level_copy)
-    sent_to_peers(wave_copy)
-    for half in (0, 1):
-        for part, toward, target in OWN_TO:
-            ring_copy(half, None, toward, target, own_part(half, part)).wait_send()
-        for slot in range(OWN):
-            for toward, target in FORWARD[slot]:
-                ring_copy(half, slot, toward, target).wait_send()
-            if slot % 2 == 0:
-                twin_copy(half, slot, core).wait_send()
-    own_twin_copy(me).wait_send()
+    levels.wait_send()
+    waves.wait_send()
+    all_of(basis.at[pl.ds(0, n // 2 * OWN // (OWN + 2)), :], ring_send, hop_recv).wait_send()
+    all_of(basis.at[pl.ds(0, n // 2), :], twin_send, hop_recv).wait_send()
 
 
 def local(angular, potential, point_rows, quanta, start_waves):
@@ -469,15 +445,15 @@
             pltpu.VMEM((solutions, 2 * width), jnp.bfloat16),
             pltpu.VMEM((chans, 8, 2 * width), jnp.float32),
             pltpu.VMEM((8, n), jnp.float32),
-            pltpu.SemaphoreType.DMA((chans,)),
-            pltpu.SemaphoreType.DMA((chans,)),
-            pltpu.SemaphoreType.DMA((chans,)),
-            pltpu.SemaphoreType.DMA((chans,)),
+            pltpu.SemaphoreType.DMA,
+            pltpu.SemaphoreType.DMA,
+            pltpu.SemaphoreType.DMA,
+            pltpu.SemaphoreType.DMA,
             pltpu.SemaphoreType.DMA((max(GROUPS),)),
             pltpu.SemaphoreType.DMA,
+            pltpu.SemaphoreType.DMA,
             pltpu.SemaphoreType.DMA((2, OWN)),
-            pltpu.SemaphoreType.DMA((2, OWN)),
-            pltpu.SemaphoreType.DMA((2, OWN // 2 + 1)),
+            pltpu.SemaphoreType.DMA,
             pltpu.SemaphoreType.DMA((2, OWN // 2 + 1)),
             pltpu.SemaphoreType.DMA((4,)),
         ],

time: 91.2 us -> 84.9 us (0.931)
  Pallas kernels: 89.1 us -> 83.3 us
    pallas_call x1, Pallas kernels: 89.1 us -> 83.3 us  [local(): pl.pallas_call(functools.partial(kernel, chans, sectors), out_shape=jax.S...]
where the time goes in v4:
time: 84.9 us; the launch traced here: 84.7 us
  Pallas kernels  83.3 us (98%)
  local copies, waits for them, and re-layouts  1.42 us (2%)
    pallas_call x1, Pallas kernels, local(): pl.pallas_call(functools.partial(kernel, chans, sectors), out_shape=jax.S...  83.3 us

profile of v4, /device:TPU:481, one launch (start us, length us, event | category | flops | bytes accessed | tf_op | source)
XLA Modules:
  0.0 84.7 jit_solution(9191389250035319512)
XLA Ops:
  0.0 83.3 %shard_map.55 = f32[2,48,64]{2,1,0:T(8,128)} custom-call(bf16[64,2048]{1,0:T(8,128)(2,1)} %bitcast.1, s32[32]{0:T(128)} %rows_ref.1, f32[32,2048]{1,0:T(8,128)} %pot_in.1, s32[2,64]{1,0:T(2,128)} %quanta_in.1, f32[48,64]{1,0:T(8,128)} %start_in.1), custom_call_target="tpu_custom_call" | custom-call | tf_op jit(solution)/shard_map/pallas_call | solution.py:424
  83.3 1.4 %copy.7 = f32[2,48,64]{2,1,0:T(8,128)} copy(f32[2,48,64]{2,1,0:T(8,128)} %shard_map.55) | data formatting | bytes 49152

commit v5 on v4

--- a/solution.py
+++ b/solution.py
@@ -14,7 +14,7 @@
 step_square = 0.08
 
 GROUPS = (2, 3, 5, 6)
-PASS_AT = (99, 99, 99, 99)
+PASS_AT = (99, 5, 9, 99)
 TILE = 512
 MESH = pl.DeviceIdType.MESH
 
@@ -53,11 +53,11 @@
 )
 ORDER = [
     ("pieces", [(-1, 0, 0), (1, 0, 1), (0, -1, 0), (0, 1, 1), (-1, 0, 1), (1, 0, 0), (0, -1, 1), (0, 1, 0)]),
-    ("levels", 0), ("take", [(0, 0)]),
+    ("take", [(0, 0)]),
     ("pieces", [(2, 0, 0), (2, 0, 1), (-1, -1, 0), (1, -1, 0), (-1, 1, 1), (1, 1, 1)]),
-    ("levels", 1), ("take", [(-1, 0), (0, -1)]),
+    ("take", [(-1, 0), (0, -1)]),
     ("pieces", [(0, 2, 0), (0, 2, 1), (-1, -1, 1), (1, -1, 1), (-1, 1, 0), (1, 1, 0)]),
-    ("take", [(1, 0), (0, 1)]),
+    ("levels", 0), ("levels", 1), ("take", [(1, 0), (0, 1)]),
     ("pieces", [(2, -1, 0), (2, 1, 1)]), ("take", [(-1, -1), (1, -1)]),
     ("pieces", [(2, -1, 1), (2, 1, 0)]), ("take", [(-1, 1), (1, 1)]),
     ("pieces", [(-1, 2, 0), (-1, 2, 1)]), ("take", [(2, 0), (0, 2)]),

time: 84.9 us -> 83 us (0.978)
  Pallas kernels: 83.3 us -> 81.4 us
    pallas_call x1, Pallas kernels: 83.3 us -> 81.4 us  [local(): pl.pallas_call(functools.partial(kernel, chans, sectors), out_shape=jax.S...]
where the time goes in v5:
time: 83 us; the launch traced here: 82.8 us
  Pallas kernels  81.4 us (98%)
  local copies, waits for them, and re-layouts  1.42 us (2%)
    pallas_call x1, Pallas kernels, local(): pl.pallas_call(functools.partial(kernel, chans, sectors), out_shape=jax.S...  81.4 us

profile of v5, /device:TPU:481, one launch (start us, length us, event | category | flops | bytes accessed | tf_op | source)
XLA Modules:
  0.0 82.8 jit_solution(18305364970196062169)
XLA Ops:
  0.0 81.4 %shard_map.55 = f32[2,48,64]{2,1,0:T(8,128)} custom-call(bf16[64,2048]{1,0:T(8,128)(2,1)} %bitcast.1, s32[32]{0:T(128)} %rows_ref.1, f32[32,2048]{1,0:T(8,128)} %pot_in.1, s32[2,64]{1,0:T(2,128)} %quanta_in.1, f32[48,64]{1,0:T(8,128)} %start_in.1), custom_call_target="tpu_custom_call" | custom-call | tf_op jit(solution)/shard_map/pallas_call | solution.py:424
  81.4 1.4 %copy.7 = f32[2,48,64]{2,1,0:T(8,128)} copy(f32[2,48,64]{2,1,0:T(8,128)} %shard_map.55) | data formatting | bytes 49152

commit v6 on v5

--- a/solution.py
+++ b/solution.py
@@ -15,7 +15,7 @@
 
 GROUPS = (2, 3, 5, 6)
 PASS_AT = (99, 5, 9, 99)
-TILE = 512
+TILE = 1024
 MESH = pl.DeviceIdType.MESH
 
 SIDE = 4
@@ -57,9 +57,9 @@
     ("pieces", [(2, 0, 0), (2, 0, 1), (-1, -1, 0), (1, -1, 0), (-1, 1, 1), (1, 1, 1)]),
     ("take", [(-1, 0), (0, -1)]),
     ("pieces", [(0, 2, 0), (0, 2, 1), (-1, -1, 1), (1, -1, 1), (-1, 1, 0), (1, 1, 0)]),
-    ("levels", 0), ("levels", 1), ("take", [(1, 0), (0, 1)]),
-    ("pieces", [(2, -1, 0), (2, 1, 1)]), ("take", [(-1, -1), (1, -1)]),
-    ("pieces", [(2, -1, 1), (2, 1, 0)]), ("take", [(-1, 1), (1, 1)]),
+    ("take", [(1, 0), (0, 1)]),
+    ("pieces", [(2, -1, 0), (2, 1, 1)]), ("levels", 0), ("take", [(-1, -1), (1, -1)]),
+    ("pieces", [(2, -1, 1), (2, 1, 0)]), ("levels", 1), ("take", [(-1, 1), (1, 1)]),
     ("pieces", [(-1, 2, 0), (-1, 2, 1)]), ("take", [(2, 0), (0, 2)]),
     ("pieces", [(1, 2, 0), (1, 2, 1)]), ("take", [(2, -1), (-1, 2)]),
     ("waves", 0), ("waves", 1), ("take", [(2, 1), (1, 2)]), ("pieces", [(2, 2, 0), (2, 2, 1)]), ("take", [(2, 2)]),

time: 83 us -> 82.9 us (level)
  no operation moved by 1% of the time
where the time goes in v6:
time: 82.9 us; the launch traced here: 82.7 us
  Pallas kernels  81.3 us (98%)
  local copies, waits for them, and re-layouts  1.42 us (2%)
    pallas_call x1, Pallas kernels, local(): pl.pallas_call(functools.partial(kernel, chans, sectors), out_shape=jax.S...  81.3 us

profile of v6, /device:TPU:481, one launch (start us, length us, event | category | flops | bytes accessed | tf_op | source)
XLA Modules:
  0.0 82.7 jit_solution(14942001547171732676)
XLA Ops:
  0.0 81.3 %shard_map.55 = f32[2,48,64]{2,1,0:T(8,128)} custom-call(bf16[64,2048]{1,0:T(8,128)(2,1)} %bitcast.1, s32[32]{0:T(128)} %rows_ref.1, f32[32,2048]{1,0:T(8,128)} %pot_in.1, s32[2,64]{1,0:T(2,128)} %quanta_in.1, f32[48,64]{1,0:T(8,128)} %start_in.1), custom_call_target="tpu_custom_call" | custom-call | tf_op jit(solution)/shard_map/pallas_call | solution.py:424
  81.3 1.4 %copy.7 = f32[2,48,64]{2,1,0:T(8,128)} copy(f32[2,48,64]{2,1,0:T(8,128)} %shard_map.55) | data formatting | bytes 49152
